TPU v7x, 128 devices: a whole 4x4x4 slice. The times are simulated.
128 devices in a mesh: dp: 4 (over y_lo, core), ctx: 32 (over y_hi, x, z).
Axes of the slice: x: 4, y: 4 (y_hi: 2, y_lo: 2; y = y_hi * 2 + y_lo), z: 4, core: 2. Of those that a mesh axis runs over, the one named last changes fastest.
Arguments:
- tokens: bfloat16 [4, 4096, 1152], P('dp', 'ctx'), may hold values from -6 to 6
- grad_out: bfloat16 [4, 4096, 1152], P('dp', 'ctx'), may hold values from -6 to 6
- pair_order: int32 [32], replicated, may hold values from 0 to 31, each once
- attn_gain: bfloat16 [1152], P(('dp', 'ctx')), may hold values from 0.5 to 1.5
- query_weight: bfloat16 [1152, 1152], P(('dp', 'ctx')), may hold values from -0.1875 to 0.1875
- key_weight: bfloat16 [1152, 384], P(('dp', 'ctx')), may hold values from -0.1875 to 0.1875
- value_weight: bfloat16 [1152, 384], P(('dp', 'ctx')), may hold values from -0.1875 to 0.1875
- output_weight: bfloat16 [1152, 1152], P(('dp', 'ctx')), may hold values from -4 to 4
- ffn_gain: bfloat16 [1152], P(('dp', 'ctx')), may hold values from 0.5 to 1.5
- gate_weight: bfloat16 [1152, 3072], P(('dp', 'ctx')), may hold values from -0.1875 to 0.1875
- up_weight: bfloat16 [1152, 3072], P(('dp', 'ctx')), may hold values from -0.1875 to 0.1875
- down_weight: bfloat16 [1152, 3072], P(('dp', 'ctx')), may hold values from -0.109375 to 0.109375
Outputs:
- block_out: bfloat16 [4, 4096, 1152], P('dp', 'ctx')
- grad_tokens: bfloat16 [4, 4096, 1152], P('dp', 'ctx')
- grad_attn_gain: float32 [1152], P(('dp', 'ctx'))
- grad_query_weight: float32 [1152, 1152], P(('dp', 'ctx'))
- grad_key_weight: float32 [1152, 384], P(('dp', 'ctx'))
- grad_value_weight: float32 [1152, 384], P(('dp', 'ctx'))
- grad_output_weight: float32 [1152, 1152], P(('dp', 'ctx'))
- grad_ffn_gain: float32 [1152], P(('dp', 'ctx'))
- grad_gate_weight: float32 [1152, 3072], P(('dp', 'ctx'))
- grad_up_weight: float32 [1152, 3072], P(('dp', 'ctx'))
- grad_down_weight: float32 [1152, 3072], P(('dp', 'ctx'))
Inputs may be any that keep to these rules, and one draw needn't show every extreme that they name: A permutation of 0 to 31; index i of ctx holds the position blocks pair_order[i] and 63 - pair_order[i] of 64 positions each, in this order.
All inputs are finite; a program needn't handle non-finite values.
Results may differ from a plain program's by a relative error of at most 0.02.
Values may be sent and summed in bfloat16 or wider, within the bound.
No kernel may reach another device: no remote copies, remote signals or barrier semaphores. Data moves between devices by JAX's collectives and lax.ppermute only.
A program may use at most 256 MiB of HBM per device.

v0:
```python
import jax
import jax.numpy as jnp
from jax import lax
from jax.sharding import PartitionSpec as P

HEAD = 64


epsilon = 1e-05


def rms_parts(inputs, gain):
    inverse = lax.rsqrt(jnp.mean(inputs * inputs, axis=-1, keepdims=True) + epsilon)
    scaled = inputs * inverse
    return (scaled * gain, scaled, inverse)


def rms_back(grad_normed, scaled, inverse, gain):
    gain_grad = jnp.sum(grad_normed * scaled, axis=0)
    grad_scaled = grad_normed * gain
    grad_inputs = inverse * (
        grad_scaled - scaled * jnp.mean(grad_scaled * scaled, axis=-1, keepdims=True)
    )
    return (grad_inputs, gain_grad)


def rope_tables(positions, width):
    half_width = width // 2
    inverse = 1.0 / 10000.0 ** (jnp.arange(half_width, dtype=jnp.float32) * (2.0 / width))
    angles = positions.astype(jnp.float32)[:, None] * inverse[None, :]
    return (jnp.cos(angles)[:, None, :], jnp.sin(angles)[:, None, :])


def rotate(vectors, cos_table, sin_table):
    half_width = vectors.shape[-1] // 2
    front_half = vectors[..., :half_width]
    back_half = vectors[..., half_width:]
    return jnp.concatenate(
        [
            front_half * cos_table - back_half * sin_table,
            back_half * cos_table + front_half * sin_table,
        ],
        axis=-1,
    )


def unrotate(gradients, cos_table, sin_table):
    half_width = gradients.shape[-1] // 2
    front_half = gradients[..., :half_width]
    back_half = gradients[..., half_width:]
    return jnp.concatenate(
        [
            front_half * cos_table + back_half * sin_table,
            back_half * cos_table - front_half * sin_table,
        ],
        axis=-1,
    )


def score_block(queries, key_rows, query_pos):
    count = queries.shape[0]
    grouped = queries.reshape(count, key_rows.shape[1], -1, queries.shape[2])
    raw_scores = jnp.einsum(
        "qkgd,tkd->kgqt", grouped, key_rows, preferred_element_type=jnp.float32
    ) * HEAD ** (-0.5)
    allowed = jnp.arange(key_rows.shape[0], dtype=jnp.int32)[None, :] <= query_pos[:, None]
    return (jnp.where(allowed, raw_scores, -1e30), grouped)


def attend_forward(queries, key_rows, value_rows, query_pos):
    scores, grouped = score_block(queries, key_rows, query_pos)
    row_max = jnp.max(scores, axis=-1, keepdims=True)
    exponent = jnp.exp(scores - row_max)
    row_total = jnp.sum(exponent, axis=-1, keepdims=True)
    attn_prob = exponent / row_total
    attended = jnp.einsum(
        "kgqt,tkd->qkgd",
        attn_prob.astype(jnp.bfloat16),
        value_rows,
        preferred_element_type=jnp.float32,
    )
    return (attended.reshape(queries.shape[0], -1), row_max + jnp.log(row_total))


def attend_backward(queries, key_rows, value_rows, query_pos, log_total, grad_attended):
    scores, grouped = score_block(queries, key_rows, query_pos)
    attn_prob = jnp.exp(scores - log_total)
    grad_grouped = grad_attended.reshape(grouped.shape)
    grad_prob = jnp.einsum(
        "qkgd,tkd->kgqt", grad_grouped, value_rows, preferred_element_type=jnp.float32
    )
    grad_scores = (
        attn_prob * (grad_prob - jnp.sum(attn_prob * grad_prob, axis=-1, keepdims=True))
    ).astype(jnp.bfloat16)
    grad_queries = jnp.einsum(
        "kgqt,tkd->qkgd", grad_scores, key_rows, preferred_element_type=jnp.float32
    ) * HEAD ** (-0.5)
    grad_keys = jnp.einsum(
        "kgqt,qkgd->tkd", grad_scores, grouped, preferred_element_type=jnp.float32
    ) * HEAD ** (-0.5)
    grad_values = jnp.einsum(
        "kgqt,qkgd->tkd",
        attn_prob.astype(jnp.bfloat16),
        grad_grouped,
        preferred_element_type=jnp.float32,
    )
    return (grad_queries.reshape(queries.shape), grad_keys, grad_values)


def body(
    tokens,
    grad_out,
    pair_order,
    attn_gain,
    query_weight,
    key_weight,
    value_weight,
    output_weight,
    ffn_gain,
    gate_weight,
    up_weight,
    down_weight,
):
    attn_parts = (
        lax.all_gather(attn_gain, ("dp", "ctx"), axis=0, tiled=True),
        lax.all_gather(query_weight, ("dp", "ctx"), axis=0, tiled=True),
        lax.all_gather(key_weight, ("dp", "ctx"), axis=0, tiled=True),
        lax.all_gather(value_weight, ("dp", "ctx"), axis=0, tiled=True),
        lax.all_gather(output_weight, ("dp", "ctx"), axis=0, tiled=True),
    )
    gain_attn, full_query, full_key, full_value, full_output = attn_parts
    gain_attn = gain_attn.astype(jnp.float32)
    groups = lax.axis_size("ctx")
    tok_rows = tokens.shape[1]
    half_rows = tok_rows // 2
    my_pair = pair_order[lax.axis_index("ctx")]
    offsets = jnp.arange(half_rows, dtype=jnp.int32)
    query_pos = jnp.concatenate(
        [my_pair * half_rows + offsets, (2 * groups - 1 - my_pair) * half_rows + offsets]
    )
    block_place = jnp.stack([pair_order, 2 * groups - 1 - pair_order], axis=1).reshape(2 * groups)
    block_index = jnp.arange(2 * groups, dtype=jnp.int32)
    matches = block_place[None, :] == block_index[:, None]
    block_source = jnp.sum(jnp.where(matches, block_index[None, :], 0), axis=1)
    inputs = tokens[0].astype(jnp.float32)
    normed_a, scaled_a, inverse_a = rms_parts(inputs, gain_attn)
    normed_a = normed_a.astype(jnp.bfloat16)
    query_proj = jnp.dot(normed_a, full_query, preferred_element_type=jnp.float32)
    key_proj = jnp.dot(normed_a, full_key, preferred_element_type=jnp.float32)
    value_proj = jnp.dot(normed_a, full_value, preferred_element_type=jnp.float32).astype(
        jnp.bfloat16
    )
    kv_width = key_proj.shape[1]
    kv_heads = kv_width // HEAD
    cos_table, sin_table = rope_tables(query_pos, HEAD)
    query_rot = rotate(query_proj.reshape(tok_rows, -1, HEAD), cos_table, sin_table).astype(
        jnp.bfloat16
    )
    key_rot = (
        rotate(key_proj.reshape(tok_rows, kv_heads, HEAD), cos_table, sin_table)
        .astype(jnp.bfloat16)
        .reshape(tok_rows, kv_width)
    )
    gathered_keys, gathered_values = (
        lax.all_gather(key_rot, "ctx", axis=0, tiled=True),
        lax.all_gather(value_proj, "ctx", axis=0, tiled=True),
    )
    key_sorted = jnp.take(
        gathered_keys.reshape(2 * groups, half_rows, kv_width), block_source, axis=0
    ).reshape(2 * groups * half_rows, kv_heads, HEAD)
    value_sorted = jnp.take(
        gathered_values.reshape(2 * groups, half_rows, kv_width), block_source, axis=0
    ).reshape(2 * groups * half_rows, kv_heads, HEAD)
    window = groups * half_rows
    early_out, early_log = attend_forward(
        query_rot[:half_rows], key_sorted[:window], value_sorted[:window], query_pos[:half_rows]
    )
    late_out, late_log = attend_forward(
        query_rot[half_rows:], key_sorted, value_sorted, query_pos[half_rows:]
    )
    attended = jnp.concatenate([early_out, late_out], axis=0).astype(jnp.bfloat16)
    hidden_one = inputs + jnp.einsum(
        "tq,dq->td", attended, full_output, preferred_element_type=jnp.float32
    )
    ffn_parts = (
        lax.all_gather(ffn_gain, ("dp", "ctx"), axis=0, tiled=True),
        lax.all_gather(gate_weight, ("dp", "ctx"), axis=0, tiled=True),
        lax.all_gather(up_weight, ("dp", "ctx"), axis=0, tiled=True),
        lax.all_gather(down_weight, ("dp", "ctx"), axis=0, tiled=True),
    )
    gain_ffn, full_gate, full_up, full_down = ffn_parts
    gain_ffn = gain_ffn.astype(jnp.float32)
    normed_f, scaled_f, inverse_f = rms_parts(hidden_one, gain_ffn)
    normed_f = normed_f.astype(jnp.bfloat16)
    gate = jnp.dot(normed_f, full_gate, preferred_element_type=jnp.float32)
    up_proj = jnp.dot(normed_f, full_up, preferred_element_type=jnp.float32)
    sigmoid_gate = jax.nn.sigmoid(gate)
    activated = gate * sigmoid_gate
    hidden = (activated * up_proj).astype(jnp.bfloat16)
    block_out = hidden_one + jnp.einsum(
        "tf,df->td", hidden, full_down, preferred_element_type=jnp.float32
    )
    grad_rows = grad_out[0]
    down_grad = jnp.einsum("td,tf->df", grad_rows, hidden, preferred_element_type=jnp.float32)
    grad_hidden = jnp.dot(grad_rows, full_down, preferred_element_type=jnp.float32)
    grad_gate = (grad_hidden * up_proj * sigmoid_gate * (1.0 + gate * (1.0 - sigmoid_gate))).astype(
        jnp.bfloat16
    )
    grad_up = (grad_hidden * activated).astype(jnp.bfloat16)
    gate_grad = jnp.einsum("td,tf->df", normed_f, grad_gate, preferred_element_type=jnp.float32)
    up_grad = jnp.einsum("td,tf->df", normed_f, grad_up, preferred_element_type=jnp.float32)
    grad_normed_f = jnp.einsum(
        "tf,df->td", grad_gate, full_gate, preferred_element_type=jnp.float32
    ) + jnp.einsum("tf,df->td", grad_up, full_up, preferred_element_type=jnp.float32)
    grad_from_ffn, ffn_gain_grad = rms_back(grad_normed_f, scaled_f, inverse_f, gain_ffn)
    grad_hidden_one = grad_rows.astype(jnp.float32) + grad_from_ffn
    ffn_sums = (
        lax.psum_scatter(ffn_gain_grad, ("dp", "ctx"), scatter_dimension=0, tiled=True),
        lax.psum_scatter(gate_grad, ("dp", "ctx"), scatter_dimension=0, tiled=True),
        lax.psum_scatter(up_grad, ("dp", "ctx"), scatter_dimension=0, tiled=True),
        lax.psum_scatter(down_grad, ("dp", "ctx"), scatter_dimension=0, tiled=True),
    )
    grad_branch = grad_hidden_one.astype(jnp.bfloat16)
    output_grad = jnp.einsum("td,tq->dq", grad_branch, attended, preferred_element_type=jnp.float32)
    grad_attended = jnp.dot(grad_branch, full_output, preferred_element_type=jnp.float32).astype(
        jnp.bfloat16
    )
    early_dq, early_dk, early_dv = attend_backward(
        query_rot[:half_rows],
        key_sorted[:window],
        value_sorted[:window],
        query_pos[:half_rows],
        early_log,
        grad_attended[:half_rows],
    )
    late_dq, late_dk, late_dv = attend_backward(
        query_rot[half_rows:],
        key_sorted,
        value_sorted,
        query_pos[half_rows:],
        late_log,
        grad_attended[half_rows:],
    )
    padding = ((0, window), (0, 0), (0, 0))
    key_grad_sorted = late_dk + jnp.pad(early_dk, padding)
    value_grad_sorted = late_dv + jnp.pad(early_dv, padding)
    key_grad_stored = jnp.take(
        key_grad_sorted.reshape(2 * groups, half_rows, kv_width), block_place, axis=0
    ).reshape(2 * groups * half_rows, kv_width)
    value_grad_stored = jnp.take(
        value_grad_sorted.reshape(2 * groups, half_rows, kv_width), block_place, axis=0
    ).reshape(2 * groups * half_rows, kv_width)
    key_grad_mine, value_grad_mine = (
        lax.psum_scatter(
            key_grad_stored.astype(jnp.bfloat16), "ctx", scatter_dimension=0, tiled=True
        ).astype(jnp.float32),
        lax.psum_scatter(
            value_grad_stored.astype(jnp.bfloat16), "ctx", scatter_dimension=0, tiled=True
        ).astype(jnp.float32),
    )
    query_grad_rot = jnp.concatenate([early_dq, late_dq], axis=0)
    grad_query = (
        unrotate(query_grad_rot, cos_table, sin_table).reshape(tok_rows, -1).astype(jnp.bfloat16)
    )
    grad_key = (
        unrotate(key_grad_mine.reshape(tok_rows, kv_heads, HEAD), cos_table, sin_table)
        .reshape(tok_rows, kv_width)
        .astype(jnp.bfloat16)
    )
    grad_value = value_grad_mine.astype(jnp.bfloat16)
    query_grad = jnp.einsum("td,tq->dq", normed_a, grad_query, preferred_element_type=jnp.float32)
    key_grad = jnp.einsum("td,tq->dq", normed_a, grad_key, preferred_element_type=jnp.float32)
    value_grad = jnp.einsum("td,tq->dq", normed_a, grad_value, preferred_element_type=jnp.float32)
    grad_normed_a = jnp.einsum(
        "tq,dq->td", grad_query, full_query, preferred_element_type=jnp.float32
    )
    grad_normed_a = grad_normed_a + jnp.einsum(
        "tq,dq->td", grad_key, full_key, preferred_element_type=jnp.float32
    )
    grad_normed_a = grad_normed_a + jnp.einsum(
        "tq,dq->td", grad_value, full_value, preferred_element_type=jnp.float32
    )
    grad_from_attn, attn_gain_grad = rms_back(grad_normed_a, scaled_a, inverse_a, gain_attn)
    grad_inputs = (grad_hidden_one + grad_from_attn).astype(jnp.bfloat16)
    attn_sums = (
        lax.psum_scatter(attn_gain_grad, ("dp", "ctx"), scatter_dimension=0, tiled=True),
        lax.psum_scatter(query_grad, ("dp", "ctx"), scatter_dimension=0, tiled=True),
        lax.psum_scatter(key_grad, ("dp", "ctx"), scatter_dimension=0, tiled=True),
        lax.psum_scatter(value_grad, ("dp", "ctx"), scatter_dimension=0, tiled=True),
        lax.psum_scatter(output_grad, ("dp", "ctx"), scatter_dimension=0, tiled=True),
    )
    return (
        block_out.astype(jnp.bfloat16)[None],
        grad_inputs[None],
        attn_sums[0],
        attn_sums[1],
        attn_sums[2],
        attn_sums[3],
        attn_sums[4],
        ffn_sums[0],
        ffn_sums[1],
        ffn_sums[2],
        ffn_sums[3],
    )


def solution(mesh):
    placed = (
        P("dp", "ctx", None),
        P("dp", "ctx", None),
        P(),
        P(("dp", "ctx")),
        P(("dp", "ctx"), None),
        P(("dp", "ctx"), None),
        P(("dp", "ctx"), None),
        P(("dp", "ctx"), None),
        P(("dp", "ctx")),
        P(("dp", "ctx"), None),
        P(("dp", "ctx"), None),
        P(("dp", "ctx"), None),
    )
    return jax.shard_map(
        body,
        mesh=mesh,
        in_specs=placed,
        out_specs=(
            P("dp", "ctx", None),
            P("dp", "ctx", None),
            P(("dp", "ctx")),
            P(("dp", "ctx"), None),
            P(("dp", "ctx"), None),
            P(("dp", "ctx"), None),
            P(("dp", "ctx"), None),
            P(("dp", "ctx")),
            P(("dp", "ctx"), None),
            P(("dp", "ctx"), None),
            P(("dp", "ctx"), None),
        ),
        check_vma=False,
    )
```

profile of v0, /device:TPU:6, one launch (start us, length us, event | category | flops | bytes accessed | tf_op | source)
XLA Modules:
  0.0 2858.7 jit_solution(4902167694712649182)
XLA Ops:
  13.0 66.2 %all-reduce.15 = (bf16[1152]{0:T(1024)(128)(2,1)S(1)}, bf16[1152]{0:T(1024)(128)(2,1)S(1)}) all-reduce(bf16[1152]{0:T(1024)(128)(2,1)S(1)} %dynamic-update-slice, bf16[1152]{0:T(1024)(128)(2,1)S(1)} %dynamic-update-slice.1), channel_id=1, replica_groups=mesh['dp'=4,'ctx'=32] {'dp','ctx'}, use_global_device_ids=true, to_apply=%add.2 | all-reduce | flops 2304 | bytes 9216
  79.2 348.7 %all-gather.1 = bf16[128,9,384]{2,1,0:T(8,128)(2,1)S(1)} all-gather(bf16[1,9,384]{2,1,0:T(8,128)(2,1)} %bitcast.277), channel_id=1, replica_groups=mesh['dp'=4,'ctx'=32] {'dp','ctx'}, dimensions={0}, use_global_device_ids=true | all-gather | bytes 891648 | tf_op jit(solution)/shard_map/all_gather | solution.py:127
  431.1 359.4 %all-gather = bf16[128,9,384]{2,1,0:T(8,128)(2,1)S(1)} all-gather(bf16[1,9,384]{2,1,0:T(8,128)(2,1)S(1)} %bitcast.278), channel_id=1, replica_groups=mesh['dp'=4,'ctx'=32] {'dp','ctx'}, dimensions={0}, use_global_device_ids=true | all-gather | bytes 891648 | tf_op jit(solution)/shard_map/all_gather | solution.py:128
  821.2 53.6 %all-gather.15.cloned.1.call-done = bf16[4096,384]{1,0:T(8,128)(2,1)} async-done(((bf16[128,384]{1,0:T(8,128)(2,1)}), bf16[4096,384]{1,0:T(8,128)(2,1)}) %all-gather.15.cloned.1.call-update) | async-done | bytes 3145744 | tf_op jit(solution)/shard_map/all_gather | solution.py:166
  885.9 10.3 copy.95
  897.5 9.5 copy.94
  924.6 7.9 reshape.383
  932.5 10.1 reshape.384
  949.4 8.1 fusion.93
  957.5 9.2 fusion.3
  972.5 8.8 fusion.48
  983.5 210.4 %all-gather.23.cloned.1.call-done = bf16[128,9,3072]{2,1,0:T(8,128)(2,1)} async-done(((bf16[1,9,3072]{2,1,0:T(8,128)(2,1)}), bf16[128,9,3072]{2,1,0:T(8,128)(2,1)}) %all-gather.23.cloned.1.call-update) | async-done | bytes 7077904 | tf_op jit(solution)/shard_map/all_gather | solution.py:187
  1193.9 13.7 reshape.367
  1207.6 309.7 %all-gather.25.cloned.1.call-done = bf16[128,9,3072]{2,1,0:T(8,128)(2,1)} async-done(((bf16[1,9,3072]{2,1,0:T(8,128)(2,1)}), bf16[128,9,3072]{2,1,0:T(8,128)(2,1)}) %all-gather.25.cloned.1.call-update) | async-done | bytes 7077904 | tf_op jit(solution)/shard_map/all_gather | solution.py:188
  1517.3 13.8 reshape.369
  1539.1 301.9 %all-gather.27.cloned.1.call-done = bf16[128,9,3072]{2,1,0:T(8,128)(2,1)} async-done(((bf16[1,9,3072]{2,1,0:T(8,128)(2,1)}), bf16[128,9,3072]{2,1,0:T(8,128)(2,1)}) %all-gather.27.cloned.1.call-update) | async-done | bytes 7077904 | tf_op jit(solution)/shard_map/all_gather | solution.py:189
  1840.9 13.9 reshape.371
  1871.4 7.2 fusion.27
  1884.7 16.8 fusion
  1901.5 9.7 bitcast_add_fusion
  1911.2 7.9 reshape.314
  1919.1 8.1 copy.103
  1927.2 7.4 fusion.9
  1936.8 13.3 fusion.2
  1957.3 9.7 reshape.311
  1967.0 9.2 copy.99
  2009.9 7.1 fusion.100
  2016.9 7.1 fusion.99
  2031.1 186.3 %reduce-scatter.4.cloned.1.call-done = bf16[128,384]{1,0:T(8,128)(2,1)} async-done(((bf16[4096,384]{1,0:T(8,128)(2,1)}), bf16[128,384]{1,0:T(8,128)(2,1)}) %reduce-scatter.4.cloned.1.call-update) | async-done | bytes 98320 | tf_op jit(solution)/shard_map/reduce_scatter | solution.py:254
  2220.2 225.6 %reduce-scatter.6.cloned.1.call-done = bf16[128,384]{1,0:T(8,128)(2,1)} async-done(((bf16[4096,384]{1,0:T(8,128)(2,1)}), bf16[128,384]{1,0:T(8,128)(2,1)}) %reduce-scatter.6.cloned.1.call-update) | async-done | bytes 98320 | tf_op jit(solution)/shard_map/reduce_scatter | solution.py:257
  2458.7 63.9 %all-reduce.13 = (f32[1152]{0:T(1024)S(1)}, f32[1152]{0:T(1024)S(1)}) all-reduce(f32[1152]{0:T(1024)S(1)} %get-tuple-element.70, f32[1152]{0:T(1024)S(1)} %get-tuple-element.68), channel_id=4, replica_groups=mesh['dp'=4,'ctx'=32] {'dp','ctx'}, use_global_device_ids=true, to_apply=%region_14.17.clone | all-reduce | flops 2304 | bytes 18432
  2524.7 314.3 %all-reduce.18.cloned.1.call-done = (f32[1152,1152]{1,0:T(8,128)}, f32[1152,384]{1,0:T(8,128)}, f32[1152,384]{1,0:T(8,128)}, f32[1152,1152]{1,0:T(8,128)}, f32[1...) async-done(((f32[1152,1152]{1,0:T(8,128)}, f32[1152,384]{1,0:T(8,128)}, f32[1152,384]{1,0:T(8,128)}, f32[1152,1152]{1,0:T(8,128)}, ...) | async-done | bytes 56623120
  (248 shorter events, 193.4 us)
Async XLA Ops:
  7.2 422.2 %copy-start.6 = (bf16[1,128,1152]{2,1,0:T(8,128)(2,1)S(1)}, bf16[1,128,1152]{2,1,0:T(8,128)(2,1)}, u32[]{:S(2)}) copy-start(bf16[1,128,1152]{2,1,0:T(8,128)(2,1)} %param.16) | copy-start | bytes 884740
  7.2 423.9 %copy-start.52 = (bf16[9,384]{1,0:T(8,128)(2,1)S(1)}, bf16[9,384]{1,0:T(8,128)(2,1)}, u32[]{:S(2)}) copy-start(bf16[9,384]{1,0:T(8,128)(2,1)} %param.22) | copy-start | bytes 20740
  7.2 792.0 %all-gather.19.cloned.1.call-start = ((), (), s32[]{:S(2)}) async-start(), calls=%async_computation.6 | async-start | bytes 4755456 | tf_op jit(solution)/shard_map/all_gather | solution.py:126
  7.9 799.2 %all-gather.21.cloned.1.call-start = ((), (), s32[]{:S(2)}) async-start(), calls=%async_computation.7 | async-start | bytes 4755456 | tf_op jit(solution)/shard_map/all_gather | solution.py:129
  8.7 808.0 %all-gather.17.cloned.1.call-start = ((), (), s32[]{:S(2)}) async-start(), calls=%async_computation.3 | async-start | bytes 3244032 | tf_op jit(solution)/shard_map/all_gather | solution.py:165
  79.2 733.8 %copy-start.47 = (f32[1152]{0:T(1024)}, f32[1152]{0:T(1024)S(1)}, u32[]{:S(2)}) copy-start(f32[1152]{0:T(1024)S(1)} %convert_element_type.137) | copy-start | bytes 13828
  428.3 365.5 %copy-start.22 = (bf16[1152,384]{1,0:T(8,128)(2,1)}, bf16[1152,384]{1,0:T(8,128)(2,1)S(1)}, u32[]{:S(2)}) copy-start(bf16[1152,384]{1,0:T(8,128)(2,1)S(1)} %reshape.361) | copy-start | bytes 2654212
  428.3 367.7 %copy-start.54 = (s32[32]{0:T(128)S(1)}, s32[32]{0:T(128)}, u32[]{:S(2)}) copy-start(s32[32]{0:T(128)} %param.18) | copy-start | bytes 388
  429.5 383.5 %copy-start.50 = (f32[128]{0:T(128)}, f32[128]{0:T(128)S(1)}, u32[]{:S(2)}) copy-start(f32[128]{0:T(128)S(1)} %add_rsqrt_fusion.1) | copy-start | bytes 1540
  429.6 386.0 %copy-start.43 = (f32[128,32]{0,1:T(8,128)}, f32[128,32]{0,1:T(8,128)S(1)}, u32[]{:S(2)}) copy-start(f32[128,32]{0,1:T(8,128)S(1)} %get-tuple-element.98) | copy-start | bytes 49156
  429.7 386.0 %copy-start.45 = (f32[128,32]{0,1:T(8,128)}, f32[128,32]{0,1:T(8,128)S(1)}, u32[]{:S(2)}) copy-start(f32[128,32]{0,1:T(8,128)S(1)} %get-tuple-element.99) | copy-start | bytes 49156
  431.0 443.8 %all-gather.15.cloned.1.call-start = ((), (), s32[]{:S(2)}) async-start(), calls=%async_computation.2 | async-start | bytes 3244032 | tf_op jit(solution)/shard_map/all_gather | solution.py:166
  793.8 400.1 %all-gather.23.cloned.1.call-start = ((), (), s32[]{:S(2)}) async-start(), calls=%async_computation.8 | async-start | bytes 12681216 | tf_op jit(solution)/shard_map/all_gather | solution.py:187
  794.4 722.9 %all-gather.25.cloned.1.call-start = ((), (), s32[]{:S(2)}) async-start(), calls=%async_computation.9 | async-start | bytes 12681216 | tf_op jit(solution)/shard_map/all_gather | solution.py:188
  795.0 1045.9 %all-gather.27.cloned.1.call-start = ((), (), s32[]{:S(2)}) async-start(), calls=%async_computation.10 | async-start | bytes 12681216 | tf_op jit(solution)/shard_map/all_gather | solution.py:189
  795.7 1421.7 %reduce-scatter.4.cloned.1.call-start = ((), (), s32[]{:S(2)}) async-start(), calls=%async_computation.4 | async-start | bytes 3244032 | tf_op jit(solution)/shard_map/reduce_scatter | solution.py:254
  803.6 9.4 copy-start.9
  932.5 16.9 copy-start.3
  957.5 9.2 copy-start.24
  972.5 8.9 copy-start.37
  972.5 8.9 copy-start.7
  983.5 553.1 %copy-start.17 = (bf16[128,1152]{1,0:T(8,128)(2,1)}, bf16[128,1152]{1,0:T(8,128)(2,1)S(1)}, u32[]{:S(2)}) copy-start(bf16[128,1152]{1,0:T(8,128)(2,1)S(1)} %multiply_convert_fusion.3) | copy-start | bytes 884740
  1840.9 26.7 slice-start.3
  1854.8 12.8 slice-start.4
  1861.6 8.6 copy-start.33
  1870.5 8.1 copy-start.19
  1870.5 8.1 slice-start
  1884.7 16.8 copy-start.15
  1936.8 17.0 copy-start.30
  1990.6 455.1 %reduce-scatter.6.cloned.1.call-start = ((), (), s32[]{:S(2)}) async-start(), calls=%async_computation.5 | async-start | bytes 3244032 | tf_op jit(solution)/shard_map/reduce_scatter | solution.py:257
  1991.4 847.6 %all-reduce.18.cloned.1.call-start = ((), (), s32[]{:S(2)}) async-start(), calls=%async_computation.11 | async-start | bytes 113246208
  2451.1 72.7 %copy-start.21 = (f32[128,1152]{1,0:T(8,128)S(1)}, f32[128,1152]{1,0:T(8,128)}, u32[]{:S(2)}) copy-start(f32[128,1152]{1,0:T(8,128)} %copy-done.19) | copy-start | bytes 1769476
  (38 other events, 191.0 us)
Sparse Core Ops, SparseCore 0:
  9.7 310.8 all-gather.18
  322.3 308.4 all-gather.20
  634.4 77.1 all-gather.16
  793.9 80.7 all-gather.14
  876.3 317.5 all-gather.22
  1195.5 321.8 all-gather.24
  1519.0 321.8 all-gather.26
  1990.8 226.5 reduce-scatter.3
  2222.4 223.2 reduce-scatter.5
  2452.1 386.8 all-reduce.17
where the time goes:
time: 2870 us; the launch traced here: 2860 us
  waiting for transfers between devices  1610 us (56%)
  blocking collectives  838 us (29%)
  local copies, waits for them, and re-layouts  198 us (7%)
  matrix products  152 us (5%)
  other arithmetic  47.8 us (2%)
    all_gather x1, blocking collectives, body(): lax.all_gather(value_weight, ('dp', 'ctx'), axis=0, tiled=True)  359 us
    all_gather x1, blocking collectives, body(): lax.all_gather(key_weight, ('dp', 'ctx'), axis=0, tiled=True)  349 us
    unnamed x11, waiting for transfers between devices  318 us
    all_gather x1, waiting for transfers between devices, body(): lax.all_gather(up_weight, ('dp', 'ctx'), axis=0, tiled=True)  310 us
    all_gather x1, waiting for transfers between devices, body(): lax.all_gather(down_weight, ('dp', 'ctx'), axis=0, tiled=True)  302 us
    reduce_scatter x1, waiting for transfers between devices, body(): lax.psum_scatter(value_grad_stored.astype(jnp.bfloat16), 'ctx', scatter_d...  226 us
    all_gather x1, waiting for transfers between devices, body(): lax.all_gather(gate_weight, ('dp', 'ctx'), axis=0, tiled=True)  210 us
    reduce_scatter x1, waiting for transfers between devices, body(): lax.psum_scatter(key_grad_stored.astype(jnp.bfloat16), 'ctx', scatter_dim...  186 us
  transfers between devices with their start and end apart: 10, of which 7 were waited for; matrix products, arithmetic and copies ran while one was open for 8% of the time, Pallas kernels for 0%

commit v1 on v0

v1 whole, which is shorter than its diff:
```python
import functools
import itertools

import jax
import jax.numpy as jnp
from jax import lax
from jax.experimental import pallas as pl
from jax.experimental.pallas import tpu as pltpu
from jax.sharding import PartitionSpec as P

ALL = ("dp", "ctx")
EPS = 1e-05
DIM = 1152
HEAD = 64
HALF_Q = 576
KV = 384
QKV = 1024
FF_PART = 768
TILE = 256
BF = jnp.bfloat16
F32 = jnp.float32


def flat(l, c, h, x, z):
    return (2 * l + c) * 32 + (4 * h + x) * 4 + z


def moves(target):
    places = itertools.product(range(2), range(2), range(2), range(4), range(4))
    return [(flat(*place), flat(*target(*place))) for place in places]


def send(value, target):
    return lax.ppermute(value, ALL, moves(target))


def to_z(step):
    return lambda l, c, h, x, z: (l, c, h, x, (z + step) % 4)


def to_x(step):
    return lambda l, c, h, x, z: (l, c, h, (x + step) % 4, z)


def to_y(step):
    def target(l, c, h, x, z):
        y = (2 * h + l + step) % 4
        return (y % 2, c, y // 2, x, z)

    return target


def other_core(l, c, h, x, z):
    return (l, 1 - c, h, x, z)


def other_h(l, c, h, x, z):
    return (l, c, 1 - h, x, z)


def z_pair(l, c, h, x, z):
    return (l, c, h, x, z ^ 1)


def home(l, c, h, x, z):
    return (l, z // 2, h, x, 2 * c + z % 2)


def home_pair(l, c, h, x, z):
    return (l, z // 2, h, x, 2 * c + 1 - z % 2)


def swap_halves(block):
    lane = lax.broadcasted_iota(jnp.int32, block.shape, 1) % HEAD
    return jnp.where(
        lane < HEAD // 2, pltpu.roll(block, 128 - HEAD // 2, 1), pltpu.roll(block, HEAD // 2, 1)
    )


def qkv_kernel(rows_ref, order_ref, weight_ref, gain_ref, cos_ref, sin_ref, x_ref, normed_ref, q_ref, kv_ref):
    inputs = jnp.dot(rows_ref[...], order_ref[...], preferred_element_type=F32)
    x_ref[...] = inputs
    inverse = lax.rsqrt(jnp.mean(inputs * inputs, axis=-1, keepdims=True) + EPS)
    normed = (inputs * inverse * gain_ref[...]).astype(BF)
    normed_ref[...] = normed
    proj = jnp.dot(normed, weight_ref[...], preferred_element_type=F32)
    cos_table, sin_table = cos_ref[...], sin_ref[...]
    for start in range(0, QKV, 128):
        block = proj[:, start : start + 128]
        turned = block * cos_table + swap_halves(block) * sin_table
        if start < 512:
            q_ref[:, start : start + 128] = (turned * 0.125).astype(BF)
        elif start == 512:
            q_ref[:, 512:576] = (turned[:, :64] * 0.125).astype(BF)
        elif start == 640:
            kv_ref[:, 0:128] = turned.astype(BF)
        elif start == 768:
            lane = lax.broadcasted_iota(jnp.int32, block.shape, 1)
            kv_ref[:, 128:256] = jnp.where(lane < HEAD, turned, block).astype(BF)
        else:
            kv_ref[:, 256:384] = block.astype(BF)


def stack_heads(block, kv_head, upper):
    parts = []
    for group in range(3):
        start = (kv_head * 3 + group) * HEAD
        parts.append(block[:, start : start + HEAD])
    rows = jnp.concatenate(parts, axis=0)
    zeros = jnp.zeros_like(rows)
    return jnp.concatenate([zeros, rows] if upper else [rows, zeros], axis=1)


K_GROUP = (0, 0, 128)
K_UPPER = (False, True, False)
V_GROUP = (128, 256, 256)
V_UPPER = (True, False, True)
NT = (((1,), (1,)), ((), ()))
TN = (((0,), (0,)), ((), ()))


def mask_tile(scores, place, tile):
    row = lax.broadcasted_iota(jnp.int32, scores.shape, 0) % 64 + place * 64
    key = lax.broadcasted_iota(jnp.int32, scores.shape, 1) + tile * TILE
    return jnp.where(key <= row, scores, -1e30)


def attend_kernel(source_ref, place_ref, q_ref, kv_ref, out_ref, log_ref, sorted_ref, score_ref):
    def put(index, carry):
        origin = pl.multiple_of(source_ref[index] * 64, 64)
        here = pl.multiple_of(index * 64, 64)
        sorted_ref[pl.ds(here, 64), :] = kv_ref[pl.ds(origin, 64), :]
        return carry

    lax.fori_loop(0, 64, put, 0)
    for block in range(4):
        place = place_ref[block]
        last = (place * 64) // TILE
        rows = q_ref[block * 64 : block * 64 + 64, :]
        queries = [stack_heads(rows, head, K_UPPER[head]) for head in range(3)]

        def score(tile, carry, masked):
            start = pl.multiple_of(tile * TILE, TILE)
            result = []
            for head in range(3):
                keys = sorted_ref[pl.ds(start, TILE), K_GROUP[head] : K_GROUP[head] + 128]
                scores = lax.dot_general(queries[head], keys, NT, preferred_element_type=F32)
                if masked:
                    scores = mask_tile(scores, place, tile)
                score_ref[head, tile] = scores
                result.append(
                    jnp.maximum(carry[head], jnp.maximum(scores[:, :128], scores[:, 128:]))
                )
            return tuple(result)

        least = tuple(jnp.full((192, 128), -1e30, F32) for _ in range(3))
        top = lax.fori_loop(0, last, functools.partial(score, masked=False), least)
        top = score(last, top, True)
        row_max = [jnp.max(part, axis=1, keepdims=True) for part in top]

        def weigh(tile, carry):
            totals, sums = carry
            start = pl.multiple_of(tile * TILE, TILE)
            next_totals, next_sums = [], []
            for head in range(3):
                values = sorted_ref[pl.ds(start, TILE), V_GROUP[head] : V_GROUP[head] + 128]
                weights = jnp.exp(score_ref[head, tile] - row_max[head])
                next_totals.append(totals[head] + weights[:, :128] + weights[:, 128:])
                next_sums.append(
                    sums[head] + jnp.dot(weights.astype(BF), values, preferred_element_type=F32)
                )
            return (tuple(next_totals), tuple(next_sums))

        zeros = tuple(jnp.zeros((192, 128), F32) for _ in range(3))
        totals, sums = lax.fori_loop(0, last + 1, weigh, (zeros, zeros))
        for head in range(3):
            row_total = jnp.sum(totals[head], axis=1, keepdims=True)
            result = sums[head] / row_total
            side = result[:, 64:] if V_UPPER[head] else result[:, :64]
            for group in range(3):
                start = (head * 3 + group) * HEAD
                out_ref[block * 64 : block * 64 + 64, start : start + HEAD] = side[
                    group * 64 : group * 64 + 64
                ]
            log_ref[block, head] = jnp.broadcast_to(row_max[head] + jnp.log(row_total), (192, 128))


def attend_back_kernel(
    spot_ref, place_ref, q_ref, sorted_ref, out_ref, log_ref, grad_ref, dq_ref, dkv_ref, total_ref
):
    total_ref[...] = jnp.zeros_like(total_ref)
    for block in range(4):
        place = place_ref[block]
        last = (place * 64) // TILE
        here = slice(block * 64, block * 64 + 64)
        rows, grads, outs = q_ref[here, :], grad_ref[here, :], out_ref[here, :]
        products = grads.astype(F32) * outs
        queries, grad_rows, deltas, logs = [], [], [], []
        for head in range(3):
            queries.append(stack_heads(rows, head, K_UPPER[head]))
            grad_rows.append(stack_heads(grads, head, V_UPPER[head]))
            deltas.append(
                jnp.sum(stack_heads(products, head, False), axis=1, keepdims=True)
            )
            logs.append(log_ref[block, head][:, :1])

        def step(tile, carry, masked):
            start = pl.multiple_of(tile * TILE, TILE)
            span = pl.ds(start, TILE)
            result = []
            for head in range(3):
                k_lanes = slice(K_GROUP[head], K_GROUP[head] + 128)
                v_lanes = slice(V_GROUP[head], V_GROUP[head] + 128)
                keys = sorted_ref[span, k_lanes]
                values = sorted_ref[span, v_lanes]
                scores = lax.dot_general(queries[head], keys, NT, preferred_element_type=F32)
                if masked:
                    scores = mask_tile(scores, place, tile)
                prob = jnp.exp(scores - logs[head])
                grad_prob = lax.dot_general(grad_rows[head], values, NT, preferred_element_type=F32)
                grad_scores = (prob * (grad_prob - deltas[head])).astype(BF)
                total_ref[span, v_lanes] += lax.dot_general(
                    prob.astype(BF), grad_rows[head], TN, preferred_element_type=F32
                )
                total_ref[span, k_lanes] += lax.dot_general(
                    grad_scores, queries[head], TN, preferred_element_type=F32
                )
                result.append(
                    carry[head] + jnp.dot(grad_scores, keys, preferred_element_type=F32)
                )
            return tuple(result)

        zeros = tuple(jnp.zeros((192, 128), F32) for _ in range(3))
        dq = lax.fori_loop(0, last, functools.partial(step, masked=False), zeros)
        dq = step(last, dq, True)
        for head in range(3):
            side = dq[head][:, 64:] if K_UPPER[head] else dq[head][:, :64]
            for group in range(3):
                start = (head * 3 + group) * HEAD
                dq_ref[here, start : start + HEAD] = side[group * 64 : group * 64 + 64] * 0.125

    def put(index, carry):
        origin = pl.multiple_of(spot_ref[index] * 64, 64)
        there = pl.multiple_of(index * 64, 64)
        dkv_ref[pl.ds(there, 64), :] = total_ref[pl.ds(origin, 64), :].astype(BF)
        return carry

    lax.fori_loop(0, 64, put, 0)


def unrotate_kernel(dq_ref, dkv_ref, cos_ref, sin_ref, out_ref):
    cos_table, sin_table = cos_ref[...], sin_ref[...]

    def turn(block):
        return block * cos_table - swap_halves(block) * sin_table

    for start in range(0, 512, 128):
        out_ref[:, start : start + 128] = turn(dq_ref[:, start : start + 128]).astype(BF)
    tail = dq_ref[:, 512:576]
    wide = jnp.concatenate([tail, jnp.zeros_like(tail)], axis=1)
    out_ref[:, 512:640] = turn(wide).astype(BF)
    out_ref[:, 640:768] = turn(dkv_ref[:, 0:128]).astype(BF)
    block = dkv_ref[:, 128:256]
    lane = lax.broadcasted_iota(jnp.int32, block.shape, 1)
    out_ref[:, 768:896] = jnp.where(lane < HEAD, turn(block), block).astype(BF)
    out_ref[:, 896:1024] = dkv_ref[:, 256:384].astype(BF)


VMEM = pl.BlockSpec(memory_space=pltpu.VMEM)
SMEM = pl.BlockSpec(memory_space=pltpu.SMEM)
ROOM = pltpu.CompilerParams(vmem_limit_bytes=48 * 1024 * 1024)


def project(rows, order, weight, gain, cos_table, sin_table):
    return pl.pallas_call(
        qkv_kernel,
        out_shape=(
            jax.ShapeDtypeStruct((256, DIM), F32),
            jax.ShapeDtypeStruct((256, DIM), BF),
            jax.ShapeDtypeStruct((256, HALF_Q), BF),
            jax.ShapeDtypeStruct((256, KV), BF),
        ),
        in_specs=[VMEM] * 6,
        out_specs=(VMEM,) * 4,
        compiler_params=ROOM,
    )(rows, order, weight, gain, cos_table, sin_table)


def attend(source, place, queries, kv):
    return pl.pallas_call(
        attend_kernel,
        out_shape=(
            jax.ShapeDtypeStruct((256, HALF_Q), F32),
            jax.ShapeDtypeStruct((4, 3, 192, 128), F32),
            jax.ShapeDtypeStruct((4096, KV), BF),
        ),
        in_specs=[SMEM, SMEM, VMEM, VMEM],
        out_specs=(VMEM,) * 3,
        scratch_shapes=[pltpu.VMEM((3, 16, 192, TILE), F32)],
        compiler_params=ROOM,
    )(source, place, queries, kv)


def attend_back(spot, place, queries, kv, out, logs, grad):
    return pl.pallas_call(
        attend_back_kernel,
        out_shape=(
            jax.ShapeDtypeStruct((256, HALF_Q), F32),
            jax.ShapeDtypeStruct((4096, KV), BF),
        ),
        in_specs=[SMEM, SMEM] + [VMEM] * 5,
        out_specs=(VMEM,) * 2,
        scratch_shapes=[pltpu.VMEM((4096, KV), F32)],
        compiler_params=ROOM,
    )(spot, place, queries, kv, out, logs, grad)


def unrotate(dq, dkv, cos_table, sin_table):
    return pl.pallas_call(
        unrotate_kernel,
        out_shape=jax.ShapeDtypeStruct((256, QKV), BF),
        in_specs=[VMEM] * 4,
        out_specs=VMEM,
        compiler_params=ROOM,
    )(dq, dkv, cos_table, sin_table)


def pick(matrix, value):
    return jnp.dot(matrix, value, preferred_element_type=F32).astype(BF)


def gather_y(pieces, z_order, y_order):
    part = pick(z_order, jnp.concatenate(pieces, axis=0))
    parts = [part] + [send(part, to_y(step)) for step in (1, 2, 3)]
    return pick(y_order, jnp.concatenate(parts, axis=0))


def gather_x(block):
    half = jnp.concatenate([block] + [send(block, to_x(step)) for step in (1, 2, 3)], axis=0)
    return jnp.concatenate([half, send(half, other_core)], axis=0)


def add_up(parts):
    total = parts[0].astype(F32)
    for part in parts[1:]:
        total = total + part.astype(F32)
    return total


def scatter(value, z_order, y_order):
    count = value.shape[0] // 2
    half = add_up([value[:count], send(value[count:].astype(BF), other_core)])
    quarter = half.reshape(4, 144, half.shape[1])
    low = quarter[1:].astype(BF)
    block = add_up([quarter[0]] + [send(low[step - 1], to_x(-step)) for step in (1, 2, 3)])
    spread = jnp.dot(y_order.T, block.astype(BF), preferred_element_type=F32).astype(BF)
    spread = spread.reshape(4, 48, -1)
    part = add_up([spread[0]] + [send(spread[step], to_y(-step)) for step in (1, 2, 3)])
    pieces = jnp.dot(z_order.T, part.astype(BF), preferred_element_type=F32).astype(BF)
    pieces = pieces.reshape(4, 16, -1)
    return [pieces[0]] + [send(pieces[step], to_z(-step)) for step in (1, 2, 3)]


def rms_parts(inputs, gain):
    inverse = lax.rsqrt(jnp.mean(inputs * inputs, axis=-1, keepdims=True) + EPS)
    scaled = inputs * inverse
    return (scaled * gain, scaled, inverse)


def rms_back(grad_normed, scaled, inverse, gain):
    gain_terms = grad_normed * scaled
    grad_scaled = grad_normed * gain
    grad_inputs = inverse * (
        grad_scaled - scaled * jnp.mean(grad_scaled * scaled, axis=-1, keepdims=True)
    )
    return (grad_inputs, gain_terms)


def rope_tables(positions):
    lane = jnp.arange(128, dtype=jnp.int32)
    inverse = 1.0 / 10000.0 ** ((lane % 32).astype(F32) * (2.0 / HEAD))
    angles = positions.astype(F32)[:, None] * inverse[None, :]
    sign = jnp.where(lane % HEAD < HEAD // 2, -1.0, 1.0)
    return (jnp.cos(angles), jnp.sin(angles) * sign[None, :])


def one_hot(rows, columns):
    return (rows == columns).astype(BF)


def body(
    tokens,
    grad_out,
    pair_order,
    attn_gain,
    query_weight,
    key_weight,
    value_weight,
    output_weight,
    ffn_gain,
    gate_weight,
    up_weight,
    down_weight,
):
    dp, ctx = lax.axis_index("dp"), lax.axis_index("ctx")
    l, c = dp // 2, dp % 2
    h, x, z = ctx // 16, (ctx // 4) % 4, ctx % 4
    y, b = 2 * h + l, z % 2
    even = b == 0

    local = jnp.arange(DIM, dtype=jnp.int32)
    from_c = (local // 576) ^ c
    from_x = (x - (local // 144) % 4) % 4
    from_y = (y - (local // 36) % 4) % 4
    from_z = (local // 9) % 4
    owner = (2 * (from_y % 2) + from_c) * 32 + (4 * (from_y // 2) + from_x) * 4 + from_z
    natural = owner * 9 + local % 9
    order = one_hot(jnp.arange(DIM, dtype=jnp.int32)[:, None], natural[None, :])
    rows48 = jnp.arange(48, dtype=jnp.int32)
    z_column = jnp.where(rows48 < 36, ((z - rows48 // 9) % 4) * 16 + rows48 % 9, -1)
    z_order = one_hot(z_column[:, None], jnp.arange(64, dtype=jnp.int32)[None, :])
    rows144 = jnp.arange(144, dtype=jnp.int32)
    y_order = one_hot(
        ((rows144 // 36) * 48 + rows144 % 36)[:, None], jnp.arange(192, dtype=jnp.int32)[None, :]
    )
    chunk = jnp.arange(64, dtype=jnp.int32)
    chunk_ctx = (
        ((chunk // 4) % 2 ^ h) * 16
        + ((x - (chunk // 8) % 4) % 4) * 4
        + 2 * ((chunk // 32) ^ c)
        + ((chunk // 2) % 2 ^ b)
    )
    ctx_match = chunk_ctx[:, None] == jnp.arange(32, dtype=jnp.int32)[None, :]
    chunk_pair = jnp.sum(jnp.where(ctx_match, pair_order[None, :], 0), axis=1)
    spot = jnp.where(chunk % 2 == 0, chunk_pair, 63 - chunk_pair)
    source = jnp.sum(jnp.where(spot[None, :] == chunk[:, None], chunk[None, :], 0), axis=1)
    place = spot[:4]
    positions = (place[:, None] * 64 + jnp.arange(64, dtype=jnp.int32)[None, :]).reshape(256)
    cos_table, sin_table = rope_tables(positions)

    rows_own = send(tokens[0], home)
    rows_pair = send(tokens[0], home_pair)

    def half_weights(side):
        return jnp.concatenate(
            [
                query_weight[:, side * 576 : side * 576 + 576],
                attn_gain[:, None],
                ffn_gain[:, None],
                jnp.zeros((9, 62), BF),
                key_weight[:, side * 192 : side * 192 + 192],
                value_weight[:, side * 192 : side * 192 + 192],
            ],
            axis=1,
        )

    rows_pad = ((0, 7), (0, 0))
    side_zero, side_one = half_weights(0), half_weights(1)
    mine = jnp.pad(jnp.where(even, side_zero, side_one), rows_pad)
    other = jnp.pad(jnp.where(even, side_one, side_zero), rows_pad)
    qkv_pieces = [
        mine,
        send(other, to_z(1)),
        send(mine, to_z(2)),
        send(other, to_z(3)),
    ]
    qkv_weight = gather_x(gather_y(qkv_pieces, z_order, y_order))
    gain_rows = jnp.einsum(
        "kc,dc->kd",
        one_hot(576 + jnp.arange(2, dtype=jnp.int32)[:, None], jnp.arange(QKV, dtype=jnp.int32)[None, :]),
        qkv_weight,
        preferred_element_type=F32,
    )
    gain_attn, gain_ffn = gain_rows[0:1], gain_rows[1:2]

    def slice_weights(step):
        start = ((z + step) % 4) * FF_PART
        parts = [
            lax.dynamic_slice_in_dim(weight, start, FF_PART, 1)
            for weight in (gate_weight, up_weight, down_weight)
        ]
        return jnp.pad(jnp.concatenate(parts + [output_weight], axis=1), rows_pad)

    ffn_pieces = [slice_weights(0)] + [send(slice_weights(step), to_z(step)) for step in (1, 2, 3)]
    ffn_weights = gather_x(gather_y(ffn_pieces, z_order, y_order))
    gate_part = ffn_weights[:, 0:768]
    up_part = ffn_weights[:, 768:1536]
    down_part = ffn_weights[:, 1536:2304]
    full_output = ffn_weights[:, 2304:3456]

    inputs, normed_a, queries, kv_own = project(
        jnp.concatenate([rows_own, rows_pair], axis=0),
        order,
        qkv_weight,
        gain_attn,
        cos_table,
        sin_table,
    )
    kv = jnp.concatenate([kv_own, send(kv_own, other_h)], axis=0)
    kv = jnp.concatenate([kv] + [send(kv, to_x(step)) for step in (1, 2, 3)], axis=0)
    kv = jnp.concatenate([kv, send(kv, other_core)], axis=0)
    heads_out, logs, kv_sorted = attend(source, place, queries, kv)
    heads_low = heads_out.astype(BF)

    grad_own = send(grad_out[0], home)
    ffn_rows = jnp.concatenate([rows_own, grad_own], axis=1)
    ffn_rows = [ffn_rows] + [send(ffn_rows, to_z(step)) for step in (1, 2, 3)]
    ffn_rows = jnp.concatenate(ffn_rows, axis=0)
    ffn_inputs = jnp.dot(ffn_rows[:, :DIM], order, preferred_element_type=F32)
    grad_rows = pick_columns(ffn_rows[:, DIM:], order)
    heads_all = [heads_low] + [send(heads_low, to_z(step)) for step in (1, 2, 3)]

    def whole_rows(low_from, upper_from, low_own):
        low = heads_all[low_from][:128] if low_own else heads_all[low_from][128:]
        upper = heads_all[upper_from][128:] if low_own else heads_all[upper_from][:128]
        return jnp.concatenate([low, upper], axis=1)

    attended = jnp.where(
        even,
        jnp.concatenate(
            [
                whole_rows(0, 3, True),
                whole_rows(2, 1, False),
                whole_rows(2, 1, True),
                whole_rows(0, 3, False),
            ],
            axis=0,
        ),
        jnp.concatenate(
            [
                whole_rows(1, 0, False),
                whole_rows(1, 0, True),
                whole_rows(3, 2, False),
                whole_rows(3, 2, True),
            ],
            axis=0,
        ),
    )
    hidden_one = ffn_inputs + jnp.einsum(
        "tq,dq->td", attended, full_output, preferred_element_type=F32
    )
    normed_f, scaled_f, inverse_f = rms_parts(hidden_one, gain_ffn)
    normed_f = normed_f.astype(BF)
    gate = jnp.dot(normed_f, gate_part, preferred_element_type=F32)
    up_proj = jnp.dot(normed_f, up_part, preferred_element_type=F32)
    sigmoid_gate = jax.nn.sigmoid(gate)
    activated = gate * sigmoid_gate
    hidden = (activated * up_proj).astype(BF)
    out_terms = jnp.einsum("tf,df->td", hidden, down_part, preferred_element_type=F32)
    grad_hidden = jnp.dot(grad_rows, down_part, preferred_element_type=F32)
    grad_gate = (grad_hidden * up_proj * sigmoid_gate * (1.0 + gate * (1.0 - sigmoid_gate))).astype(BF)
    grad_up = (grad_hidden * activated).astype(BF)
    grad_normed_f = jnp.einsum(
        "tf,df->td", grad_gate, gate_part, preferred_element_type=F32
    ) + jnp.einsum("tf,df->td", grad_up, up_part, preferred_element_type=F32)

    def sum_rows(terms):
        low = terms[128:].astype(BF).reshape(3, 128, DIM)
        return add_up([terms[:128]] + [send(low[step - 1], to_z(-step)) for step in (1, 2, 3)])

    grad_from_ffn, ffn_gain_terms = rms_back(
        sum_rows(grad_normed_f), scaled_f[:128], inverse_f[:128], gain_ffn
    )
    grad_hidden_one = grad_rows[:128].astype(F32) + grad_from_ffn
    grad_branch = grad_hidden_one.astype(BF)
    grad_branch = jnp.concatenate([grad_branch, send(grad_branch, z_pair)], axis=0)
    block_out = (hidden_one[:128] + sum_rows(out_terms)).astype(BF)
    block_out = send(unpick_columns(block_out, order), home)

    output_part = jnp.where(even, full_output[:, :576], full_output[:, 576:])
    grad_heads = jnp.dot(grad_branch, output_part, preferred_element_type=F32).astype(BF)
    output_grad = jnp.einsum("td,tq->dq", grad_branch, heads_low, preferred_element_type=F32)
    dq, dkv = attend_back(spot, place, queries, kv_sorted, heads_out, logs, grad_heads)

    down_grad = jnp.einsum("td,tf->df", grad_rows, hidden, preferred_element_type=F32)
    gate_grad = jnp.einsum("td,tf->df", normed_f, grad_gate, preferred_element_type=F32)
    up_grad = jnp.einsum("td,tf->df", normed_f, grad_up, preferred_element_type=F32)
    ffn_grads = jnp.concatenate([gate_grad, up_grad, down_grad], axis=1)
    ffn_pieces = scatter(ffn_grads, z_order, y_order)

    dkv = add_up([dkv[:2048], send(dkv[2048:], other_core)])
    dkv = dkv.reshape(4, 512, KV)
    low = dkv[1:].astype(BF)
    dkv = add_up([dkv[0]] + [send(low[step - 1], to_x(-step)) for step in (1, 2, 3)])
    dkv = add_up([dkv[:256], send(dkv[256:].astype(BF), other_h)])
    grad_qkv = unrotate(dq, dkv, cos_table, sin_table)
    qkv_grad = jnp.einsum("td,tq->dq", normed_a, grad_qkv, preferred_element_type=F32)
    grad_normed_a = jnp.einsum("tq,dq->td", grad_qkv, qkv_weight, preferred_element_type=F32)
    grad_normed_a = grad_normed_a[:128] + send(grad_normed_a[128:].astype(BF), z_pair).astype(F32)
    _, scaled_a, inverse_a = rms_parts(inputs[:128], gain_attn)
    grad_from_attn, attn_gain_terms = rms_back(grad_normed_a, scaled_a, inverse_a, gain_attn)
    grad_inputs = (grad_hidden_one + grad_from_attn).astype(BF)
    grad_inputs = send(unpick_columns(grad_inputs, order), home)

    lanes = jnp.arange(QKV, dtype=jnp.int32)[None, :]
    gain_grads = jnp.einsum(
        "td,tk->dk",
        jnp.concatenate([attn_gain_terms, ffn_gain_terms], axis=0).astype(BF),
        one_hot(576 + jnp.arange(256, dtype=jnp.int32)[:, None] // 128, lanes),
        preferred_element_type=F32,
    )
    attn_pieces = scatter(
        jnp.concatenate([qkv_grad + gain_grads, output_grad], axis=1), z_order, y_order
    )

    from_mine = add_up([attn_pieces[0], attn_pieces[2]])[:9]
    from_other = add_up([attn_pieces[1], attn_pieces[3]])[:9]
    side_zero = jnp.where(even, from_mine, from_other)
    side_one = jnp.where(even, from_other, from_mine)

    def both(start, count):
        return jnp.concatenate(
            [side_zero[:, start : start + count], side_one[:, start : start + count]], axis=1
        )

    attn_gain_grad = side_zero[:, 576] + side_one[:, 576]
    ffn_gain_grad = side_zero[:, 577] + side_one[:, 577]
    stacked = jnp.stack(ffn_pieces)[:, :9].astype(F32)

    def whole(start):
        slices = [
            lax.dynamic_index_in_dim(stacked, (part - z) % 4, 0, keepdims=False)[:, start : start + 768]
            for part in range(4)
        ]
        return jnp.concatenate(slices, axis=1)

    return (
        block_out[None],
        grad_inputs[None],
        attn_gain_grad,
        both(0, 576),
        both(640, 192),
        both(832, 192),
        both(1024, 576),
        ffn_gain_grad,
        whole(0),
        whole(768),
        whole(1536),
    )


def pick_columns(rows, order):
    return jnp.dot(rows, order, preferred_element_type=F32).astype(BF)


def unpick_columns(rows, order):
    return jnp.einsum("tk,dk->td", rows, order, preferred_element_type=F32).astype(BF)


def solution(mesh):
    weights = P(ALL, None)
    rows = P("dp", "ctx", None)
    return jax.shard_map(
        body,
        mesh=mesh,
        in_specs=(rows, rows, P(), P(ALL), weights, weights, weights, weights, P(ALL), weights, weights, weights),
        out_specs=(rows, rows, P(ALL), weights, weights, weights, weights, P(ALL), weights, weights, weights),
        check_vma=False,
    )
```

time: 2870 us -> 479 us (0.17)
  waiting for transfers between devices: 1610 us -> 191 us
  blocking collectives: 838 us -> 0 us
  local copies, waits for them, and re-layouts: 198 us -> 29 us
  matrix products: 152 us -> 46.3 us
  starting transfers between devices: 0.6 us -> 89.9 us
  Pallas kernels: 0 us -> 85.3 us
    all_gather x7 -> x0, waiting for transfers between devices: 876 us -> none  [the longest x1 310 us: body(): lax.all_gather(up_weight, ('dp', 'ctx'), axis=0, tiled=True)]
    all_gather x2 -> x0, blocking collectives: 708 us -> none  [the longest x1 359 us: body(): lax.all_gather(value_weight, ('dp', 'ctx'), axis=0, tiled=True)]
    reduce_scatter x2 -> x0, waiting for transfers between devices: 412 us -> none  [the longest x1 226 us: body(): lax.psum_scatter(value_grad_stored.astype(jnp.bfloat16), 'ctx', scatter_d...]
    unnamed x11 -> x0, waiting for transfers between devices: 318 us -> none
    ppermute x0 -> x69, waiting for transfers between devices: none -> 191 us  [send(): return lax.ppermute(value, ALL, moves(target))]
    unnamed x2 -> x0, blocking collectives: 130 us -> none
    dot_general x33 -> x28, matrix products: 152 us -> 46.3 us  [the longest x2 6.46 us: unpick_columns(): jnp.einsum('tk,dk->td', rows, order, preferred_element_type=F32).astype(BF)]
    ppermute x0 -> x69, starting transfers between devices: none -> 89.9 us  [send(): return lax.ppermute(value, ALL, moves(target))]
  transfers between devices with their start and end apart: 10 -> 69, of which waited for: 7 -> 39; matrix products, arithmetic and copies ran while one was open for 8% -> 13% of each run, Pallas kernels for 0% -> 8%
where the time goes in v1:
time: 479 us; the launch traced here: 475 us
  waiting for transfers between devices  191 us (40%)
  starting transfers between devices  89.9 us (19%)
  Pallas kernels  85.3 us (18%)
  matrix products  46.3 us (10%)
  other arithmetic  31.6 us (7%)
  local copies, waits for them, and re-layouts  29 us (6%)
    ppermute x69, waiting for transfers between devices, send(): return lax.ppermute(value, ALL, moves(target))  191 us
    ppermute x69, starting transfers between devices, send(): return lax.ppermute(value, ALL, moves(target))  89.9 us
    pallas_call x1, Pallas kernels, attend_back(): pl.pallas_call(attend_back_kernel, out_shape=(jax.ShapeDtypeStruct((256,...  46.9 us
    pallas_call x1, Pallas kernels, attend(): pl.pallas_call(attend_kernel, out_shape=(jax.ShapeDtypeStruct((256, HALF_...  33.9 us
    unnamed x95, local copies, waits for them, and re-layouts  15.5 us
    another operation x6, other arithmetic  9.7 us
  transfers between devices with their start and end apart: 69, of which 39 were waited for; matrix products, arithmetic and copies ran while one was open for 13% of the time, Pallas kernels for 8%

profile of v1, /device:TPU:6, one launch (start us, length us, event | category | flops | bytes accessed | tf_op | source)
XLA Modules:
  0.0 475.0 jit_solution(7803070410038929868)
XLA Ops:
  4.2 4.1 collective-permute-start.8
  14.2 3.6 collective-permute-start.7
  27.5 3.6 collective-permute-done.10
  36.4 5.1 %collective-permute-done.12 = bf16[144,1024]{1,0:T(8,128)(2,1)S(1)} collective-permute-done((bf16[144,1024]{1,0:T(8,128)(2,1)S(1)}, bf16[144,1024]{1,0:T(8,128)(2,1)S(1)}, u32[]{:S(2)}, u32[]{:S(2)}) %collective-permute-start.12) | collective-permute-done | bytes 294944 | tf_op jit(solution)/shard_map/ppermute | solution.py:34
  53.7 4.9 %collective-permute-done.28 = bf16[48,3456]{1,0:T(8,128)(2,1)S(1)} collective-permute-done((bf16[48,3456]{1,0:T(8,128)(2,1)S(1)}, bf16[48,3456]{1,0:T(8,128)(2,1)S(1)}, u32[]{:S(2)}, u32[]{:S(2)}) %collective-permute-start.28) | collective-permute-done | bytes 331808 | tf_op jit(solution)/shard_map/ppermute | solution.py:34
  58.6 4.8 %collective-permute-done.27 = bf16[48,3456]{1,0:T(8,128)(2,1)S(1)} collective-permute-done((bf16[48,3456]{1,0:T(8,128)(2,1)S(1)}, bf16[48,3456]{1,0:T(8,128)(2,1)S(1)}, u32[]{:S(2)}, u32[]{:S(2)}) %collective-permute-start.27) | collective-permute-done | bytes 331808 | tf_op jit(solution)/shard_map/ppermute | solution.py:34
  70.8 3.9 shard_map.203
  74.7 36.2 %collective-permute-done.30 = bf16[144,3456]{1,0:T(8,128)(2,1)S(1)} collective-permute-done((bf16[144,3456]{1,0:T(8,128)(2,1)S(1)}, bf16[144,3456]{1,0:T(8,128)(2,1)S(1)}, u32[]{:S(2)}, u32[]{:S(2)}) %collective-permute-start.30) | collective-permute-done | bytes 995360 | tf_op jit(solution)/shard_map/ppermute | solution.py:34
  115.3 5.0 %pad_maximum_fusion.1 = bf16[576,3456]{1,0:T(8,128)(2,1)S(1)} fusion(bf16[144,3456]{1,0:T(8,128)(2,1)S(1)} %collective-permute-done.32, bf16[144,3456]{1,0:T(8,128)(2,1)S(1)} %collective-permute-done.31, bf16[144,3456]{1,0:T(8,128)(2,1)S(1)} %collective-permute-done.30, bf16[144,3456]{1,0:T(8,128)(2,1)S(1)} %copy-done.35), kind=kLoop, calls=%fused_computation.14 | loop fusion | flops 15925248 | bytes 7962624 | tf_op jit(solution)/shard_map/concatenate | solution.py:339
  126.7 5.9 %collective-permute-done.17 = bf16[512,384]{1,0:T(8,128)(2,1)S(1)} collective-permute-done((bf16[512,384]{1,0:T(8,128)(2,1)S(1)}, bf16[512,384]{1,0:T(8,128)(2,1)S(1)}, u32[]{:S(2)}, u32[]{:S(2)}) %collective-permute-start.17) | collective-permute-done | bytes 393248 | tf_op jit(solution)/shard_map/ppermute | solution.py:34
  136.1 7.1 %collective-permute-done.19 = bf16[512,384]{1,0:T(8,128)(2,1)S(1)} collective-permute-done((bf16[512,384]{1,0:T(8,128)(2,1)S(1)}, bf16[512,384]{1,0:T(8,128)(2,1)S(1)}, u32[]{:S(2)}, u32[]{:S(2)}) %collective-permute-start.19) | collective-permute-done | bytes 393248 | tf_op jit(solution)/shard_map/ppermute | solution.py:34
  152.2 33.9 %shard_map.204 = (f32[256,576]{1,0:T(8,128)S(1)}, f32[4,3,192,128]{3,2,1,0:T(8,128)S(1)}, bf16[4096,384]{1,0:T(8,128)(2,1)S(1)}) custom-call(s32[64]{0:T(128)S(1)} %select_reduce_fusion.source_ref, s32[4]{0:T(128)S(1)} %get-tuple-element.151.place_ref, bf16[256,576]{1,0:T(8,128)(2,1)S(1)} %get-tuple-element.20.q_ref, bf16[4096,384]{1,0:T(8,128)(2,1)} %copy-done.20), custom_call_target="tpu_custom_call" | custom-call | tf_op jit(solution)/shard_map/pallas_call | solution.py:290
  189.9 8.4 %collective-permute-done.22 = bf16[256,576]{1,0:T(8,128)(2,1)S(1)} collective-permute-done((bf16[256,576]{1,0:T(8,128)(2,1)S(1)}, bf16[256,576]{1,0:T(8,128)(2,1)S(1)}, u32[]{:S(2)}, u32[]{:S(2)}) %collective-permute-start.22) | collective-permute-done | bytes 294944 | tf_op jit(solution)/shard_map/ppermute | solution.py:34
  198.3 6.8 %collective-permute-done.21 = bf16[256,576]{1,0:T(8,128)(2,1)S(1)} collective-permute-done((bf16[256,576]{1,0:T(8,128)(2,1)S(1)}, bf16[256,576]{1,0:T(8,128)(2,1)S(1)}, u32[]{:S(2)}, u32[]{:S(2)}) %collective-permute-start.21) | collective-permute-done | bytes 294944 | tf_op jit(solution)/shard_map/ppermute | solution.py:34
  225.6 3.7 collective-permute-start.39
  235.9 6.5 %collective-permute-done.39 = bf16[128,1152]{1,0:T(8,128)(2,1)S(1)} collective-permute-done((bf16[128,1152]{1,0:T(8,128)(2,1)S(1)}, bf16[128,1152]{1,0:T(8,128)(2,1)S(1)}, u32[]{:S(2)}, u32[]{:S(2)}) %collective-permute-start.39) | collective-permute-done | bytes 294944 | tf_op jit(solution)/shard_map/ppermute | solution.py:34
  246.9 4.7 collective-permute-done.41
  258.2 46.9 %shard_map.205 = (f32[256,576]{1,0:T(8,128)S(1)}, bf16[4096,384]{1,0:T(8,128)(2,1)}) custom-call(s32[64]{0:T(128)S(1)} %compare_select_fusion.12.spot_ref, s32[4]{0:T(128)S(1)} %get-tuple-element.151.place_ref, bf16[256,576]{1,0:T(8,128)(2,1)S(1)} %get-tuple-element.20.q_ref, bf16[4096,384]{1,0:T(8,128)(2,1)} %copy-done, ...), custom_call_target="tpu_custom_call" | custom-call | tf_op jit(solution)/shard_map/pallas_call | solution.py:305
  306.8 4.6 pad_maximum_fusion
  317.0 3.8 collective-permute-start.35
  323.1 3.9 collective-permute-done.36
  327.4 7.0 %collective-permute-done.35 = bf16[128,1152]{1,0:T(8,128)(2,1)S(1)} collective-permute-done((bf16[128,1152]{1,0:T(8,128)(2,1)S(1)}, bf16[128,1152]{1,0:T(8,128)(2,1)S(1)}, u32[]{:S(2)}, u32[]{:S(2)}) %collective-permute-start.35) | collective-permute-done | bytes 294944 | tf_op jit(solution)/shard_map/ppermute | solution.py:34
  341.4 6.3 %collective-permute-done.43 = bf16[512,384]{1,0:T(8,128)(2,1)S(1)} collective-permute-done((bf16[512,384]{1,0:T(8,128)(2,1)S(1)}, bf16[512,384]{1,0:T(8,128)(2,1)S(1)}, u32[]{:S(2)}, u32[]{:S(2)}) %collective-permute-start.43) | collective-permute-done | bytes 393248 | tf_op jit(solution)/shard_map/ppermute | solution.py:34
  350.6 3.9 fusion.209
  361.1 4.2 collective-permute-done.47
  369.0 3.8 collective-permute-start.48
  378.1 11.9 %collective-permute-done.60 = bf16[144,2304]{1,0:T(8,128)(2,1)S(1)} collective-permute-done((bf16[144,2304]{1,0:T(8,128)(2,1)S(1)}, bf16[144,2304]{1,0:T(8,128)(2,1)S(1)}, u32[]{:S(2)}, u32[]{:S(2)}) %collective-permute-start.60) | collective-permute-done | bytes 663584 | tf_op jit(solution)/shard_map/ppermute | solution.py:34
  398.8 6.6 %collective-permute-done.65 = bf16[48,2304]{1,0:T(8,128)(2,1)S(1)} collective-permute-done((bf16[48,2304]{1,0:T(8,128)(2,1)S(1)}, bf16[48,2304]{1,0:T(8,128)(2,1)S(1)}, u32[]{:S(2)}, u32[]{:S(2)}) %collective-permute-start.65) | collective-permute-done | bytes 221216 | tf_op jit(solution)/shard_map/ppermute | solution.py:34
  408.1 7.4 %collective-permute-start.67 = (bf16[16,2304]{1,0:T(8,128)(2,1)S(1)}, bf16[16,2304]{1,0:T(8,128)(2,1)}, u32[]{:S(2)}, u32[]{:S(2)}) collective-permute-start(bf16[16,2304]{1,0:T(8,128)(2,1)S(1)} %get-tuple-element.89), channel_id=1, source_target_pairs={{0,2},{1,3},{2,0},{3,1},{4,6},{5,7},{6,4},{7,5},{8,10},{9,11},{10,... | collective-permute-start | bytes 221192 | tf_op jit(solution)/shard_map/ppermute | solution.py:34
  427.4 10.4 %collective-permute-done.52 = bf16[144,1600]{1,0:T(8,128)(2,1)S(1)} collective-permute-done((bf16[144,1600]{1,0:T(8,128)(2,1)S(1)}, bf16[144,1600]{1,0:T(8,128)(2,1)S(1)}, u32[]{:S(2)}, u32[]{:S(2)}) %collective-permute-start.52) | collective-permute-done | bytes 460832 | tf_op jit(solution)/shard_map/ppermute | solution.py:34
  439.5 7.5 %collective-permute-done.50 = bf16[144,1600]{1,0:T(8,128)(2,1)S(1)} collective-permute-done((bf16[144,1600]{1,0:T(8,128)(2,1)S(1)}, bf16[144,1600]{1,0:T(8,128)(2,1)S(1)}, u32[]{:S(2)}, u32[]{:S(2)}) %collective-permute-start.50) | collective-permute-done | bytes 460832 | tf_op jit(solution)/shard_map/ppermute | solution.py:34
  454.8 4.5 collective-permute-done.54
  (330 shorter events, 192.4 us)
Async XLA Ops:
  4.2 17.4 %collective-permute-start.8 = (bf16[16,1024]{1,0:T(8,128)(2,1)S(1)}, bf16[16,1024]{1,0:T(8,128)(2,1)S(1)}, u32[]{:S(2)}, u32[]{:S(2)}) collective-permute-start(bf16[16,1024]{1,0:T(8,128)(2,1)S(1)} %pad.21), channel_id=1, source_target_pairs={{0,3},{1,0},{2,1},{3,2},{4,7},{5,4},{6,5},{7,6},{8,11},{9,8},{10,9... | collective-permute-start | bytes 98312 | tf_op jit(solution)/shard_map/ppermute | solution.py:34
  10.8 24.5 %collective-permute-start.26 = (bf16[16,3456]{1,0:T(8,128)(2,1)S(1)}, bf16[16,3456]{1,0:T(8,128)(2,1)S(1)}, u32[]{:S(2)}, u32[]{:S(2)}) collective-permute-start(bf16[16,3456]{1,0:T(8,128)(2,1)S(1)} %pad.25), channel_id=1, source_target_pairs={{0,3},{1,0},{2,1},{3,2},{4,7},{5,4},{6,5},{7,6},{8,11},{9,8},{10,9... | collective-permute-start | bytes 331784 | tf_op jit(solution)/shard_map/ppermute | solution.py:34
  14.1 21.2 %collective-permute-start.25 = (bf16[16,3456]{1,0:T(8,128)(2,1)S(1)}, bf16[16,3456]{1,0:T(8,128)(2,1)S(1)}, u32[]{:S(2)}, u32[]{:S(2)}) collective-permute-start(bf16[16,3456]{1,0:T(8,128)(2,1)S(1)} %pad.24), channel_id=1, source_target_pairs={{0,2},{1,3},{2,0},{3,1},{4,6},{5,7},{6,4},{7,5},{8,10},{9,11},{10,... | collective-permute-start | bytes 331784 | tf_op jit(solution)/shard_map/ppermute | solution.py:34
  47.1 22.4 %collective-permute-start.15 = (bf16[576,1024]{1,0:T(8,128)(2,1)S(1)}, bf16[576,1024]{1,0:T(8,128)(2,1)S(1)}, u32[]{:S(2)}, u32[]{:S(2)}) collective-permute-start(bf16[576,1024]{1,0:T(8,128)(2,1)S(1)} %pad_maximum_fusion.14), channel_id=1, source_target_pairs={{0,32},{1,33},{2,34},{3,35},{4,36},{5,37},{6,38},{7,39},{8,40},{9,... | collective-permute-start | bytes 3538952 | tf_op jit(solution)/shard_map/ppermute | solution.py:34
  47.3 16.1 %collective-permute-start.27 = (bf16[48,3456]{1,0:T(8,128)(2,1)S(1)}, bf16[48,3456]{1,0:T(8,128)(2,1)S(1)}, u32[]{:S(2)}, u32[]{:S(2)}) collective-permute-start(bf16[48,3456]{1,0:T(8,128)(2,1)S(1)} %convolution_convert_fusion.1), channel_id=1, source_target_pairs={{0,64},{1,65},{2,66},{3,67},{4,68},{5,69},{6,70},{7,71},{8,72},{9,... | collective-permute-start | bytes 995336 | tf_op jit(solution)/shard_map/ppermute | solution.py:34
  48.4 74.1 %collective-permute-start.4 = (bf16[128,2304]{1,0:T(8,128)(2,1)S(1)}, bf16[128,2304]{1,0:T(8,128)(2,1)S(1)}, u32[]{:S(2)}, u32[]{:S(2)}) collective-permute-start(bf16[128,2304]{1,0:T(8,128)(2,1)S(1)} %constant_dynamic-update-slice_fusion), channel_id=1, source_target_pairs={{0,3},{1,0},{2,1},{3,2},{4,7},{5,4},{6,5},{7,6},{8,11},{9,8},{10,9... | collective-permute-start | bytes 1769480 | tf_op jit(solution)/shard_map/ppermute | solution.py:34
  64.8 46.1 %collective-permute-start.30 = (bf16[144,3456]{1,0:T(8,128)(2,1)S(1)}, bf16[144,3456]{1,0:T(8,128)(2,1)S(1)}, u32[]{:S(2)}, u32[]{:S(2)}) collective-permute-start(bf16[144,3456]{1,0:T(8,128)(2,1)S(1)} %get-tuple-element.155), channel_id=1, source_target_pairs={{0,4},{1,5},{2,6},{3,7},{4,8},{5,9},{6,10},{7,11},{8,12},{9,13},{1... | collective-permute-start | bytes 2985992 | tf_op jit(solution)/shard_map/ppermute | solution.py:34
  68.0 43.3 %collective-permute-start.31 = (bf16[144,3456]{1,0:T(8,128)(2,1)S(1)}, bf16[144,3456]{1,0:T(8,128)(2,1)S(1)}, u32[]{:S(2)}, u32[]{:S(2)}) collective-permute-start(bf16[144,3456]{1,0:T(8,128)(2,1)S(1)} %get-tuple-element.155), channel_id=1, source_target_pairs={{0,8},{1,9},{2,10},{3,11},{4,12},{5,13},{6,14},{7,15},{8,0},{9,1},... | collective-permute-start | bytes 2985992 | tf_op jit(solution)/shard_map/ppermute | solution.py:34
  68.0 46.3 %collective-permute-start.32 = (bf16[144,3456]{1,0:T(8,128)(2,1)S(1)}, bf16[144,3456]{1,0:T(8,128)(2,1)S(1)}, u32[]{:S(2)}, u32[]{:S(2)}) collective-permute-start(bf16[144,3456]{1,0:T(8,128)(2,1)S(1)} %get-tuple-element.155), channel_id=1, source_target_pairs={{0,12},{1,13},{2,14},{3,15},{4,0},{5,1},{6,2},{7,3},{8,4},{9,5},{1... | collective-permute-start | bytes 2985992 | tf_op jit(solution)/shard_map/ppermute | solution.py:34
  69.5 53.1 %collective-permute-start.3 = (bf16[128,2304]{1,0:T(8,128)(2,1)S(1)}, bf16[128,2304]{1,0:T(8,128)(2,1)S(1)}, u32[]{:S(2)}, u32[]{:S(2)}) collective-permute-start(bf16[128,2304]{1,0:T(8,128)(2,1)S(1)} %constant_dynamic-update-slice_fusion), channel_id=1, source_target_pairs={{0,2},{1,3},{2,0},{3,1},{4,6},{5,7},{6,4},{7,5},{8,10},{9,11},{10,... | collective-permute-start | bytes 1769480 | tf_op jit(solution)/shard_map/ppermute | solution.py:34
  110.9 15.6 %collective-permute-start.2 = (bf16[128,2304]{1,0:T(8,128)(2,1)S(1)}, bf16[128,2304]{1,0:T(8,128)(2,1)S(1)}, u32[]{:S(2)}, u32[]{:S(2)}) collective-permute-start(bf16[128,2304]{1,0:T(8,128)(2,1)S(1)} %constant_dynamic-update-slice_fusion), channel_id=1, source_target_pairs={{0,1},{1,2},{2,3},{3,0},{4,5},{5,6},{6,7},{7,4},{8,9},{9,10},{10,1... | collective-permute-start | bytes 1769480 | tf_op jit(solution)/shard_map/ppermute | solution.py:34
  120.3 84.9 %collective-permute-start.33 = (bf16[576,3456]{1,0:T(8,128)(2,1)S(1)}, bf16[576,3456]{1,0:T(8,128)(2,1)S(1)}, u32[]{:S(2)}, u32[]{:S(2)}) collective-permute-start(bf16[576,3456]{1,0:T(8,128)(2,1)S(1)} %pad_maximum_fusion.1), channel_id=1, source_target_pairs={{0,32},{1,33},{2,34},{3,35},{4,36},{5,37},{6,38},{7,39},{8,40},{9,... | collective-permute-start | bytes 11943944 | tf_op jit(solution)/shard_map/ppermute | solution.py:34
  122.4 13.5 %collective-permute-start.18 = (bf16[512,384]{1,0:T(8,128)(2,1)S(1)}, bf16[512,384]{1,0:T(8,128)(2,1)S(1)}, u32[]{:S(2)}, u32[]{:S(2)}) collective-permute-start(bf16[512,384]{1,0:T(8,128)(2,1)S(1)} %get-tuple-element.99), channel_id=1, source_target_pairs={{0,8},{1,9},{2,10},{3,11},{4,12},{5,13},{6,14},{7,15},{8,0},{9,1},... | collective-permute-start | bytes 1179656 | tf_op jit(solution)/shard_map/ppermute | solution.py:34
  122.6 20.5 %collective-permute-start.19 = (bf16[512,384]{1,0:T(8,128)(2,1)S(1)}, bf16[512,384]{1,0:T(8,128)(2,1)S(1)}, u32[]{:S(2)}, u32[]{:S(2)}) collective-permute-start(bf16[512,384]{1,0:T(8,128)(2,1)S(1)} %get-tuple-element.99), channel_id=1, source_target_pairs={{0,12},{1,13},{2,14},{3,15},{4,0},{5,1},{6,2},{7,3},{8,4},{9,5},{1... | collective-permute-start | bytes 1179656 | tf_op jit(solution)/shard_map/ppermute | solution.py:34
  186.3 18.8 %collective-permute-start.21 = (bf16[256,576]{1,0:T(8,128)(2,1)S(1)}, bf16[256,576]{1,0:T(8,128)(2,1)S(1)}, u32[]{:S(2)}, u32[]{:S(2)}) collective-permute-start(bf16[256,576]{1,0:T(8,128)(2,1)S(1)} %convert_element_type.228), channel_id=1, source_target_pairs={{0,3},{1,0},{2,1},{3,2},{4,7},{5,4},{6,5},{7,6},{8,11},{9,8},{10,9... | collective-permute-start | bytes 884744 | tf_op jit(solution)/shard_map/ppermute | solution.py:34
  189.1 16.0 %collective-permute-start.23 = (bf16[256,576]{1,0:T(8,128)(2,1)S(1)}, bf16[256,576]{1,0:T(8,128)(2,1)S(1)}, u32[]{:S(2)}, u32[]{:S(2)}) collective-permute-start(bf16[256,576]{1,0:T(8,128)(2,1)S(1)} %convert_element_type.228), channel_id=1, source_target_pairs={{0,1},{1,2},{2,3},{3,0},{4,5},{5,6},{6,7},{7,4},{8,9},{9,10},{10,1... | collective-permute-start | bytes 884744 | tf_op jit(solution)/shard_map/ppermute | solution.py:34
  225.6 16.7 %collective-permute-start.39 = (bf16[128,1152]{1,0:T(8,128)(2,1)S(1)}, bf16[128,1152]{1,0:T(8,128)(2,1)S(1)}, u32[]{:S(2)}, u32[]{:S(2)}) collective-permute-start(bf16[128,1152]{1,0:T(8,128)(2,1)S(1)} %get-tuple-element.59), channel_id=1, source_target_pairs={{0,2},{1,3},{2,0},{3,1},{4,6},{5,7},{6,4},{7,5},{8,10},{9,11},{10,... | collective-permute-start | bytes 884744 | tf_op jit(solution)/shard_map/ppermute | solution.py:34
  306.7 14.9 %collective-permute-start.42 = (bf16[2048,384]{1,0:T(8,128)(2,1)S(1)}, bf16[2048,384]{1,0:T(8,128)(2,1)S(1)}, u32[]{:S(2)}, u32[]{:S(2)}) collective-permute-start(bf16[2048,384]{1,0:T(8,128)(2,1)S(1)} %slice.427), channel_id=1, source_target_pairs={{0,32},{1,33},{2,34},{3,35},{4,36},{5,37},{6,38},{7,39},{8,40},{9,... | collective-permute-start | bytes 4718600 | tf_op jit(solution)/shard_map/ppermute | solution.py:34
  311.7 38.9 %collective-permute-start.59 = (bf16[576,2304]{1,0:T(8,128)(2,1)S(1)}, bf16[576,2304]{1,0:T(8,128)(2,1)S(1)}, u32[]{:S(2)}, u32[]{:S(2)}) collective-permute-start(bf16[576,2304]{1,0:T(8,128)(2,1)S(1)} %slice.726), channel_id=1, source_target_pairs={{0,32},{1,33},{2,34},{3,35},{4,36},{5,37},{6,38},{7,39},{8,40},{9,... | collective-permute-start | bytes 7962632 | tf_op jit(solution)/shard_map/ppermute | solution.py:34
  317.0 17.4 %collective-permute-start.35 = (bf16[128,1152]{1,0:T(8,128)(2,1)S(1)}, bf16[128,1152]{1,0:T(8,128)(2,1)S(1)}, u32[]{:S(2)}, u32[]{:S(2)}) collective-permute-start(bf16[128,1152]{1,0:T(8,128)(2,1)S(1)} %get-tuple-element.62), channel_id=1, source_target_pairs={{0,2},{1,3},{2,0},{3,1},{4,6},{5,7},{6,4},{7,5},{8,10},{9,11},{10,... | collective-permute-start | bytes 884744 | tf_op jit(solution)/shard_map/ppermute | solution.py:34
  320.7 13.7 %collective-permute-start.34 = (bf16[128,1152]{1,0:T(8,128)(2,1)S(1)}, bf16[128,1152]{1,0:T(8,128)(2,1)S(1)}, u32[]{:S(2)}, u32[]{:S(2)}) collective-permute-start(bf16[128,1152]{1,0:T(8,128)(2,1)S(1)} %get-tuple-element.60), channel_id=1, source_target_pairs={{0,3},{1,0},{2,1},{3,2},{4,7},{5,4},{6,5},{7,6},{8,11},{9,8},{10,9... | collective-permute-start | bytes 884744 | tf_op jit(solution)/shard_map/ppermute | solution.py:34
  322.2 19.3 %collective-permute-start.45 = (bf16[512,384]{1,0:T(8,128)(2,1)S(1)}, bf16[512,384]{1,0:T(8,128)(2,1)S(1)}, u32[]{:S(2)}, u32[]{:S(2)}) collective-permute-start(bf16[512,384]{1,0:T(8,128)(2,1)S(1)} %get-tuple-element.55), channel_id=1, source_target_pairs={{0,4},{1,5},{2,6},{3,7},{4,8},{5,9},{6,10},{7,11},{8,12},{9,13},{1... | collective-permute-start | bytes 1179656 | tf_op jit(solution)/shard_map/ppermute | solution.py:34
  326.9 14.5 %collective-permute-start.44 = (bf16[512,384]{1,0:T(8,128)(2,1)S(1)}, bf16[512,384]{1,0:T(8,128)(2,1)S(1)}, u32[]{:S(2)}, u32[]{:S(2)}) collective-permute-start(bf16[512,384]{1,0:T(8,128)(2,1)S(1)} %get-tuple-element.56), channel_id=1, source_target_pairs={{0,8},{1,9},{2,10},{3,11},{4,12},{5,13},{6,14},{7,15},{8,0},{9,1},... | collective-permute-start | bytes 1179656 | tf_op jit(solution)/shard_map/ppermute | solution.py:34
  337.5 77.9 %collective-permute-start.37 = (bf16[128,1152]{1,0:T(8,128)(2,1)}, bf16[128,1152]{1,0:T(8,128)(2,1)S(1)}, u32[]{:S(2)}, u32[]{:S(2)}) collective-permute-start(bf16[128,1152]{1,0:T(8,128)(2,1)} %fusion.16), channel_id=1, source_target_pairs={{0,0},{1,1},{2,32},{3,33},{4,4},{5,5},{6,36},{7,37},{8,8},{9,9},{1... | collective-permute-start | bytes 884744 | tf_op jit(solution)/shard_map/ppermute | solution.py:34
  358.5 17.9 %collective-permute-start.62 = (bf16[144,2304]{1,0:T(8,128)(2,1)S(1)}, bf16[144,2304]{1,0:T(8,128)(2,1)S(1)}, u32[]{:S(2)}, u32[]{:S(2)}) collective-permute-start(bf16[144,2304]{1,0:T(8,128)(2,1)S(1)} %get-tuple-element.49), channel_id=1, source_target_pairs={{0,4},{1,5},{2,6},{3,7},{4,8},{5,9},{6,10},{7,11},{8,12},{9,13},{1... | collective-permute-start | bytes 1990664 | tf_op jit(solution)/shard_map/ppermute | solution.py:34
  358.6 19.5 %collective-permute-start.61 = (bf16[144,2304]{1,0:T(8,128)(2,1)S(1)}, bf16[144,2304]{1,0:T(8,128)(2,1)S(1)}, u32[]{:S(2)}, u32[]{:S(2)}) collective-permute-start(bf16[144,2304]{1,0:T(8,128)(2,1)S(1)} %get-tuple-element.50), channel_id=1, source_target_pairs={{0,8},{1,9},{2,10},{3,11},{4,12},{5,13},{6,14},{7,15},{8,0},{9,1},... | collective-permute-start | bytes 1990664 | tf_op jit(solution)/shard_map/ppermute | solution.py:34
  359.5 30.4 %collective-permute-start.60 = (bf16[144,2304]{1,0:T(8,128)(2,1)S(1)}, bf16[144,2304]{1,0:T(8,128)(2,1)S(1)}, u32[]{:S(2)}, u32[]{:S(2)}) collective-permute-start(bf16[144,2304]{1,0:T(8,128)(2,1)S(1)} %get-tuple-element.48), channel_id=1, source_target_pairs={{0,12},{1,13},{2,14},{3,15},{4,0},{5,1},{6,2},{7,3},{8,4},{9,5},{1... | collective-permute-start | bytes 1990664 | tf_op jit(solution)/shard_map/ppermute | solution.py:34
  369.0 48.1 %collective-permute-start.48 = (bf16[128,1152]{1,0:T(8,128)(2,1)}, bf16[128,1152]{1,0:T(8,128)(2,1)}, u32[]{:S(2)}, u32[]{:S(2)}) collective-permute-start(bf16[128,1152]{1,0:T(8,128)(2,1)} %fusion.17), channel_id=1, source_target_pairs={{0,0},{1,1},{2,32},{3,33},{4,4},{5,5},{6,36},{7,37},{8,8},{9,9},{1... | collective-permute-start | bytes 884744 | tf_op jit(solution)/shard_map/ppermute | solution.py:34
  405.4 15.6 %collective-permute-start.49 = (bf16[576,1600]{1,0:T(8,128)(2,1)}, bf16[576,1600]{1,0:T(8,128)(2,1)}, u32[]{:S(2)}, u32[]{:S(2)}) collective-permute-start(bf16[576,1600]{1,0:T(8,128)(2,1)} %fusion.7), channel_id=1, source_target_pairs={{0,32},{1,33},{2,34},{3,35},{4,36},{5,37},{6,38},{7,39},{8,40},{9,... | collective-permute-start | bytes 5529608 | tf_op jit(solution)/shard_map/ppermute | solution.py:34
  423.9 14.0 %collective-permute-start.52 = (bf16[144,1600]{1,0:T(8,128)(2,1)S(1)}, bf16[144,1600]{1,0:T(8,128)(2,1)S(1)}, u32[]{:S(2)}, u32[]{:S(2)}) collective-permute-start(bf16[144,1600]{1,0:T(8,128)(2,1)S(1)} %get-tuple-element.52), channel_id=1, source_target_pairs={{0,4},{1,5},{2,6},{3,7},{4,8},{5,9},{6,10},{7,11},{8,12},{9,13},{1... | collective-permute-start | bytes 1382408 | tf_op jit(solution)/shard_map/ppermute | solution.py:34
  424.0 15.5 %collective-permute-start.51 = (bf16[144,1600]{1,0:T(8,128)(2,1)S(1)}, bf16[144,1600]{1,0:T(8,128)(2,1)S(1)}, u32[]{:S(2)}, u32[]{:S(2)}) collective-permute-start(bf16[144,1600]{1,0:T(8,128)(2,1)S(1)} %get-tuple-element.53), channel_id=1, source_target_pairs={{0,8},{1,9},{2,10},{3,11},{4,12},{5,13},{6,14},{7,15},{8,0},{9,1},... | collective-permute-start | bytes 1382408 | tf_op jit(solution)/shard_map/ppermute | solution.py:34
  425.4 21.5 %collective-permute-start.50 = (bf16[144,1600]{1,0:T(8,128)(2,1)S(1)}, bf16[144,1600]{1,0:T(8,128)(2,1)S(1)}, u32[]{:S(2)}, u32[]{:S(2)}) collective-permute-start(bf16[144,1600]{1,0:T(8,128)(2,1)S(1)} %get-tuple-element.51), channel_id=1, source_target_pairs={{0,12},{1,13},{2,14},{3,15},{4,0},{5,1},{6,2},{7,3},{8,4},{9,5},{1... | collective-permute-start | bytes 1382408 | tf_op jit(solution)/shard_map/ppermute | solution.py:34
  (78 other events, 914.6 us)
